TPU v7x, 256 devices: a whole 4x4x8 slice. The times are simulated.
256 devices in a mesh: pipe: 16 (over z, x_lo), expert: 16 (over y, x_hi, core).
Axes of the slice: x: 4 (x_hi: 2, x_lo: 2; x = x_hi * 2 + x_lo), y: 4, z: 8, core: 2. Of those that a mesh axis runs over, the one named last changes fastest.
Arguments:
- flight: bfloat16 [16, 2048, 4096], P('pipe', 'expert'), may hold values from -6 to 6
- norm_gain: float32 [16, 4096], P('pipe'), may hold values from 0.5 to 2
- router: bfloat16 [16, 4096, 8], P('pipe'), may hold values from -0.09375 to 0.09375
- w_gate: bfloat16 [16, 4096, 6144], P('pipe', None, 'expert'), may hold values from -0.09375 to 0.09375
- w_up: bfloat16 [16, 4096, 6144], P('pipe', None, 'expert'), may hold values from -0.09375 to 0.09375
- w_down: bfloat16 [16, 6144, 4096], P('pipe', 'expert'), may hold values from -0.21875 to 0.21875
- routes: int32 [16, 2, 2048, 2], P('pipe', None, 'expert'), may hold values from 0 to 7, all different within a row; in each aligned block of 128 rows (0 to 127, 128 to 255, ..., all dimensions but the last counted through in order) at most 48 rows name the same one
Outputs:
- landed: bfloat16 [16, 2048, 4096], P('pipe', 'expert')
Inputs may be any that keep to these rules, and one draw needn't show every extreme that they name: `routes`: each row names 2 different experts. In each aligned block of 128 rows (the rows of one device for one section and step) no expert is named by more than 48 rows, and in some block an expert is named by exactly 48 rows.
All inputs are finite; a program needn't handle non-finite values.
Results may differ from a plain program's by a relative error of at most 0.0084.
Values may be sent and summed in bfloat16 or wider, within the bound.
No kernel may reach another device: no remote copies, remote signals or barrier semaphores. Data moves between devices by JAX's collectives and lax.ppermute only.
A program may use at most 128 MiB of HBM per device.

v0:
```python
import jax
import jax.numpy as jnp
from jax import lax
from jax.sharding import PartitionSpec as P


def passed_along(value, axis, steps):
    count = lax.axis_size(axis)
    pairs = [(source, (source + steps) % count) for source in range(count)]
    return lax.ppermute(value, axis, pairs)


def build_slots(block, route_ids, experts, capacity):
    rows_local = block.shape[0]
    top_count = route_ids.shape[1]
    flat_ids = route_ids.reshape(-1)
    onehot = (flat_ids[:, None] == jnp.arange(experts, dtype=jnp.int32)[None, :]).astype(jnp.int32)
    before = jnp.cumsum(onehot, axis=0) - onehot
    position = jnp.sum(before * onehot, axis=1)
    slot_index = flat_ids * capacity + position
    source_row = jnp.arange(rows_local * top_count, dtype=jnp.int32) // top_count + 1
    slot_table = jnp.zeros((experts * capacity,), jnp.int32).at[slot_index].set(source_row)
    padded = jnp.concatenate([jnp.zeros((1, block.shape[1]), block.dtype), block], axis=0)
    return (slot_index, jnp.take(padded, slot_table, axis=0))


def half_output(rows, gate_cols, up_cols, down_rows):
    gate_act = jnp.dot(rows, gate_cols, preferred_element_type=jnp.float32)
    up_act = jnp.dot(rows, up_cols, preferred_element_type=jnp.float32)
    hidden = (jax.nn.silu(gate_act) * up_act).astype(jnp.bfloat16)
    partial_value = jnp.dot(hidden, down_rows, preferred_element_type=jnp.float32).astype(
        jnp.bfloat16
    )
    return lax.optimization_barrier(partial_value)


def body(flight, norm_gain, router, w_gate, w_up, w_down, routes):
    expert_count = lax.axis_size("expert")
    rows_local = flight.shape[1]
    model_width = flight.shape[2]
    experts = router.shape[2]
    top_count = routes.shape[3]
    capacity = 2 * min(rows_local // 2, 3 * rows_local * top_count // (4 * experts))
    current = flight[0]
    for step_index in range(routes.shape[1]):
        float_state = current.astype(jnp.float32)
        normed = (
            float_state
            * lax.rsqrt(jnp.mean(float_state * float_state, axis=-1, keepdims=True) + 1e-06)
            * norm_gain[0][None, :]
        ).astype(jnp.bfloat16)
        logits = jnp.dot(normed, router[0], preferred_element_type=jnp.float32)
        route_ids = routes[0, step_index]
        picked = route_ids[:, :, None] == jnp.arange(experts, dtype=jnp.int32)[None, None, :]
        chosen = jnp.sum(jnp.where(picked, logits[:, None, :], 0.0), axis=-1)
        raised = jnp.exp(chosen)
        mix_weight = raised / jnp.sum(raised, axis=1, keepdims=True)
        slot_index, outgoing = build_slots(normed, route_ids, experts, capacity)
        doubled = jnp.broadcast_to(
            outgoing.reshape(experts, 1, capacity, model_width), (experts, 2, capacity, model_width)
        )
        arrived = lax.all_to_all(
            doubled.reshape(expert_count, capacity, model_width),
            "expert",
            split_axis=0,
            concat_axis=0,
            tiled=True,
        )
        flat_rows = arrived.reshape(expert_count * capacity, model_width)
        partial_value = half_output(flat_rows, w_gate[0], w_up[0], w_down[0]).reshape(
            expert_count, capacity, model_width
        )
        returned = lax.all_to_all(partial_value, "expert", split_axis=0, concat_axis=0, tiled=True)
        paired = returned.reshape(experts, 2, capacity, model_width)
        expert_out = (paired[:, 0].astype(jnp.float32) + paired[:, 1].astype(jnp.float32)).astype(
            jnp.bfloat16
        )
        expert_out = expert_out.reshape(experts * capacity, model_width)
        gathered = jnp.take(expert_out, slot_index, axis=0).reshape(
            rows_local, top_count, model_width
        )
        moe = jnp.sum(mix_weight[:, :, None] * gathered.astype(jnp.float32), axis=1)
        current = (float_state + moe).astype(jnp.bfloat16)
        current = passed_along(current, "pipe", 1)
    return current[None]


def solution(mesh):
    return jax.shard_map(
        body,
        mesh=mesh,
        in_specs=(
            P("pipe", "expert", None),
            P("pipe", None),
            P("pipe", None, None),
            P("pipe", None, "expert"),
            P("pipe", None, "expert"),
            P("pipe", "expert", None),
            P("pipe", None, "expert", None),
        ),
        out_specs=P("pipe", "expert", None),
        check_vma=False,
    )
```

profile of v0, /device:TPU:12, one launch (start us, length us, event | category | flops | bytes accessed | tf_op | source)
XLA Modules:
  0.0 502.5 jit_solution(3968399123727673391)
XLA Ops:
  5.4 1.6 fusion.15
  8.3 9.6 %gather_fusion = bf16[384,4096]{1,0:T(8,128)(2,1)} fusion(bf16[129,4096]{1,0:T(8,128)(2,1)} %concatenate.6, s32[1024]{0:T(1024)S(1)} %pad_clamp_fusion.3), kind=kCustom, calls=%fused_computation.clone | custom fusion | bytes 6292992 | tf_op jit(solution)/shard_map/jit(_take)/gather | solution.py:24
  17.9 2.2 broadcast_select_fusion.1
  21.0 76.7 %all_to_all.20 = bf16[16,48,4096]{2,1,0:T(8,128)(2,1)S(1)} all-to-all(bf16[16,48,4096]{2,1,0:T(8,128)(2,1)S(1)} %bitcast.122), channel_id=1, replica_groups=mesh['pipe'=16,'expert'=16] {'expert'}, dimensions={0} | all-to-all | bytes 12582912 | tf_op jit(solution)/shard_map/all_to_all | solution.py:62
  97.7 3.4 fusion.8
  101.2 3.5 fusion.32
  104.7 5.4 %convolution_convert_fusion.1 = bf16[768,4096]{1,0:T(8,128)(2,1)} fusion(bf16[768,384]{1,0:T(8,128)(2,1)S(1)} %fusion.32, bf16[1,384,4096]{2,1,0:T(8,128)(2,1)S(1)} %copy-done), kind=kOutput, calls=%fused_computation.7 | convolution fusion | flops 2419064832 | bytes 10027008 | tf_op jit(solution)/shard_map/dot_general | solution.py:31
  110.1 10.0 %all-to-all-start.1 = ((bf16[16,48,4096]{2,1,0:T(8,128)(2,1)}), bf16[16,48,4096]{2,1,0:T(8,128)(2,1)}, u32[]{:S(2)}, u32[]{:S(2)}) async-start(bf16[16,48,4096]{2,1,0:T(8,128)(2,1)} %bitcast.126), calls=%async_computation.1 | async-start | bytes 12582912 | tf_op jit(solution)/shard_map/all_to_all | solution.py:73
  120.1 1.7 fusion.36
  122.2 67.5 %all-to-all-done.1 = bf16[16,48,4096]{2,1,0:T(8,128)(2,1)} async-done(((bf16[16,48,4096]{2,1,0:T(8,128)(2,1)}), bf16[16,48,4096]{2,1,0:T(8,128)(2,1)}, u32[]{:S(2)}, u32[]{:S(2)}) %all-to-all-start.1) | async-done | bytes 6291488 | tf_op jit(solution)/shard_map/all_to_all | solution.py:73
  189.7 5.9 %add_convert_fusion.1 = bf16[8,1,48,4096]{3,2,0,1:T(8,128)(2,1)} fusion(bf16[8,2,48,4096]{3,2,1,0:T(8,128)(2,1)} %bitcast.16), kind=kLoop, calls=%fused_computation.9 | loop fusion | flops 6291456 | bytes 9437184 | tf_op jit(solution)/shard_map/convert_element_type | solution.py:75
  195.6 7.5 %gather_fusion.1 = bf16[256,4096]{1,0:T(8,128)(2,1)} fusion(bf16[384,4096]{1,0:T(8,128)(2,1)} %bitcast.120, s32[1024]{0:T(1024)S(1)} %pad_clamp_fusion.2), kind=kCustom, calls=%fused_computation.1.clone | custom fusion | bytes 4195328 | tf_op jit(solution)/shard_map/jit(_take)/gather | solution.py:79
  203.1 3.9 select_convert_fusion.1
  206.9 6.0 %reshape.233 = f32[128,2,4096]{2,1,0:T(2,128)} reshape(f32[256,4096]{1,0:T(8,128)} %select_convert_fusion.1) | data formatting | bytes 8388608 | tf_op jit(solution)/shard_map/convert_element_type | solution.py:82
  213.0 8.8 %multiply_reduce_fusion.1 = f32[128,4096]{1,0:T(8,128)S(1)} fusion(f32[128,2,4096]{2,1,0:T(2,128)} %reshape.233, f32[128,2]{1,0:T(8,128)S(1)} %copy.30), kind=kLoop, calls=%fused_computation.11 | loop fusion | flops 1572864 | bytes 6292480 | tf_op jit(solution)/shard_map/reduce_sum | solution.py:82
  227.0 26.4 %collective-permute-done = bf16[128,4096]{1,0:T(8,128)(2,1)} collective-permute-done((bf16[128,4096]{1,0:T(8,128)(2,1)}, bf16[128,4096]{1,0:T(8,128)(2,1)}, u32[]{:S(2)}, u32[]{:S(2)}) %collective-permute-start) | collective-permute-done | bytes 1048608 | tf_op jit(solution)/shard_map/ppermute | solution.py:10
  255.0 1.6 fusion.21
  258.8 10.1 %gather_fusion.2 = bf16[384,4096]{1,0:T(8,128)(2,1)} fusion(bf16[129,4096]{1,0:T(8,128)(2,1)} %concatenate.7, s32[1024]{0:T(1024)S(1)} %pad_clamp_fusion.1), kind=kCustom, calls=%fused_computation.2.clone | custom fusion | bytes 6292992 | tf_op jit(solution)/shard_map/jit(_take)/gather | solution.py:24
  268.9 2.2 broadcast_select_fusion
  272.0 76.6 %all_to_all.21 = bf16[16,48,4096]{2,1,0:T(8,128)(2,1)S(1)} all-to-all(bf16[16,48,4096]{2,1,0:T(8,128)(2,1)S(1)} %bitcast.123), channel_id=1, replica_groups=mesh['pipe'=16,'expert'=16] {'expert'}, dimensions={0} | all-to-all | bytes 12582912 | tf_op jit(solution)/shard_map/all_to_all | solution.py:62
  348.5 3.4 fusion.6
  351.9 3.5 fusion.29
  355.5 5.4 %convolution_convert_fusion = bf16[768,4096]{1,0:T(8,128)(2,1)} fusion(bf16[768,384]{1,0:T(8,128)(2,1)S(1)} %fusion.29, bf16[1,384,4096]{2,1,0:T(8,128)(2,1)S(1)} %copy-done), kind=kOutput, calls=%fused_computation.6 | convolution fusion | flops 2419064832 | bytes 10027008 | tf_op jit(solution)/shard_map/dot_general | solution.py:31
  360.9 9.8 %all-to-all-start.3 = ((bf16[16,48,4096]{2,1,0:T(8,128)(2,1)}), bf16[16,48,4096]{2,1,0:T(8,128)(2,1)}, u32[]{:S(2)}, u32[]{:S(2)}) async-start(bf16[16,48,4096]{2,1,0:T(8,128)(2,1)} %bitcast.127), calls=%async_computation.3 | async-start | bytes 12582912 | tf_op jit(solution)/shard_map/all_to_all | solution.py:73
  370.7 1.6 fusion.40
  372.5 67.8 %all-to-all-done.3 = bf16[16,48,4096]{2,1,0:T(8,128)(2,1)} async-done(((bf16[16,48,4096]{2,1,0:T(8,128)(2,1)}), bf16[16,48,4096]{2,1,0:T(8,128)(2,1)}, u32[]{:S(2)}, u32[]{:S(2)}) %all-to-all-start.3) | async-done | bytes 6291488 | tf_op jit(solution)/shard_map/all_to_all | solution.py:73
  440.3 5.9 %add_convert_fusion = bf16[8,1,48,4096]{3,2,0,1:T(8,128)(2,1)} fusion(bf16[8,2,48,4096]{3,2,1,0:T(8,128)(2,1)} %bitcast.27), kind=kLoop, calls=%fused_computation.8 | loop fusion | flops 6291456 | bytes 9437184 | tf_op jit(solution)/shard_map/convert_element_type | solution.py:75
  446.2 7.5 %gather_fusion.3 = bf16[256,4096]{1,0:T(8,128)(2,1)} fusion(bf16[384,4096]{1,0:T(8,128)(2,1)} %bitcast.121, s32[1024]{0:T(1024)S(1)} %pad_clamp_fusion), kind=kCustom, calls=%fused_computation.3.clone | custom fusion | bytes 4195328 | tf_op jit(solution)/shard_map/jit(_take)/gather | solution.py:79
  453.7 3.9 select_convert_fusion
  457.5 6.0 %reshape.234 = f32[128,2,4096]{2,1,0:T(2,128)} reshape(f32[256,4096]{1,0:T(8,128)} %select_convert_fusion) | data formatting | bytes 8388608 | tf_op jit(solution)/shard_map/convert_element_type | solution.py:82
  463.5 8.7 %multiply_reduce_fusion = f32[128,4096]{1,0:T(8,128)S(1)} fusion(f32[128,2,4096]{2,1,0:T(2,128)} %reshape.234, f32[128,2]{1,0:T(8,128)S(1)} %copy.36), kind=kLoop, calls=%fused_computation.10 | loop fusion | flops 1572864 | bytes 6292480 | tf_op jit(solution)/shard_map/reduce_sum | solution.py:82
  473.9 27.5 %collective-permute-done.1 = bf16[128,4096]{1,0:T(8,128)(2,1)S(1)} collective-permute-done((bf16[128,4096]{1,0:T(8,128)(2,1)S(1)}, bf16[128,4096]{1,0:T(8,128)(2,1)S(1)}, u32[]{:S(2)}, u32[]{:S(2)}) %collective-permute-start.1) | collective-permute-done | bytes 1048608 | tf_op jit(solution)/shard_map/ppermute | solution.py:10
  (77 shorter events, 20.4 us)
Async XLA Ops:
  0.0 104.7 %copy-start = (bf16[1,384,4096]{2,1,0:T(8,128)(2,1)S(1)}, bf16[1,384,4096]{2,1,0:T(8,128)(2,1)}, u32[]{:S(2)}) copy-start(bf16[1,384,4096]{2,1,0:T(8,128)(2,1)} %param.16) | copy-start | bytes 9437188
  21.0 76.8 %copy-start.5 = (bf16[1,4096,384]{2,1,0:T(8,128)(2,1)S(1)}, bf16[1,4096,384]{2,1,0:T(8,128)(2,1)}, u32[]{:S(2)}) copy-start(bf16[1,4096,384]{2,1,0:T(8,128)(2,1)} %param.14) | copy-start | bytes 9437188
  97.7 3.4 copy-start.7
  110.1 10.0 %copy-start.3 = (f32[1,4096]{1,0:T(1,128)S(1)}, f32[1,4096]{1,0:T(1,128)}, u32[]{:S(2)}) copy-start(f32[1,4096]{1,0:T(1,128)} %param.12) | copy-start | bytes 49156
  110.1 10.0 %copy-start.4 = (bf16[1,4096,8]{1,2,0:T(8,128)(2,1)S(1)}, bf16[1,4096,8]{1,2,0:T(8,128)(2,1)}, u32[]{:S(2)}) copy-start(bf16[1,4096,8]{1,2,0:T(8,128)(2,1)} %param.13) | copy-start | bytes 196612
  110.1 79.6 %all-to-all-start.1 = ((bf16[16,48,4096]{2,1,0:T(8,128)(2,1)}), bf16[16,48,4096]{2,1,0:T(8,128)(2,1)}, u32[]{:S(2)}, u32[]{:S(2)}) async-start(bf16[16,48,4096]{2,1,0:T(8,128)(2,1)} %bitcast.126), calls=%async_computation.1 | async-start | bytes 12582912 | tf_op jit(solution)/shard_map/all_to_all | solution.py:73
  213.0 8.8 %copy-start.2 = (bf16[1,128,4096]{2,1,0:T(8,128)(2,1)S(1)}, bf16[1,128,4096]{2,1,0:T(8,128)(2,1)}, u32[]{:S(2)}) copy-start(bf16[1,128,4096]{2,1,0:T(8,128)(2,1)} %param.11) | copy-start | bytes 3145732
  223.0 30.4 %collective-permute-start = (bf16[128,4096]{1,0:T(8,128)(2,1)}, bf16[128,4096]{1,0:T(8,128)(2,1)}, u32[]{:S(2)}, u32[]{:S(2)}) collective-permute-start(bf16[128,4096]{1,0:T(8,128)(2,1)} %fusion.16), channel_id=1, source_target_pairs={{0,16},{16,32},{32,48},{48,64},{64,80},{80,96},{96,112},{112,128},... | collective-permute-start | bytes 3145736 | tf_op jit(solution)/shard_map/ppermute | solution.py:10
  256.5 1.0 copy-start.1
  271.9 76.6 %copy-start.6 = (bf16[1,4096,384]{2,1,0:T(8,128)(2,1)S(1)}, bf16[1,4096,384]{2,1,0:T(8,128)(2,1)}, u32[]{:S(2)}) copy-start(bf16[1,4096,384]{2,1,0:T(8,128)(2,1)} %param.14) | copy-start | bytes 9437188
  348.5 3.4 copy-start.8
  360.9 79.4 %all-to-all-start.3 = ((bf16[16,48,4096]{2,1,0:T(8,128)(2,1)}), bf16[16,48,4096]{2,1,0:T(8,128)(2,1)}, u32[]{:S(2)}, u32[]{:S(2)}) async-start(bf16[16,48,4096]{2,1,0:T(8,128)(2,1)} %bitcast.127), calls=%async_computation.3 | async-start | bytes 12582912 | tf_op jit(solution)/shard_map/all_to_all | solution.py:73
  473.8 27.5 %collective-permute-start.1 = (bf16[128,4096]{1,0:T(8,128)(2,1)S(1)}, bf16[128,4096]{1,0:T(8,128)(2,1)S(1)}, u32[]{:S(2)}, u32[]{:S(2)}) collective-permute-start(bf16[128,4096]{1,0:T(8,128)(2,1)S(1)} %fusion.22), channel_id=1, source_target_pairs={{0,16},{16,32},{32,48},{48,64},{64,80},{80,96},{96,112},{112,128},... | collective-permute-start | bytes 3145736 | tf_op jit(solution)/shard_map/ppermute | solution.py:10
where the time goes:
time: 512 us; the launch traced here: 503 us
  waiting for transfers between devices  189 us (37%)
  blocking collectives  153 us (30%)
  local copies, waits for them, and re-layouts  57.7 us (11%)
  other arithmetic  52.8 us (10%)
  matrix products  28 us (5%)
  starting transfers between devices  21 us (4%)
    all_to_all x2, blocking collectives, body(): lax.all_to_all(doubled.reshape(expert_count, capacity, model_width), 'exp...  153 us
    all_to_all x2, waiting for transfers between devices, body(): lax.all_to_all(partial_value, 'expert', split_axis=0, concat_axis=0, tile...  135 us
    ppermute x2, waiting for transfers between devices, passed_along(): return lax.ppermute(value, axis, pairs)  53.9 us
    gather x2, local copies, waits for them, and re-layouts, build_slots(): return (slot_index, jnp.take(padded, slot_table, axis=0))  19.7 us
    all_to_all x2, starting transfers between devices, body(): lax.all_to_all(partial_value, 'expert', split_axis=0, concat_axis=0, tile...  19.7 us
    reduce_sum x2, other arithmetic, body(): moe = jnp.sum(mix_weight[:, :, None] * gathered.astype(jnp.float32), axis=1)  17.6 us
    gather x2, local copies, waits for them, and re-layouts, body(): jnp.take(expert_out, slot_index, axis=0)  15 us
    convert_element_type x2, local copies, waits for them, and re-layouts, body(): moe = jnp.sum(mix_weight[:, :, None] * gathered.astype(jnp.float32), axis=1)  12 us
  transfers between devices with their start and end apart: 4, of which 4 were waited for; matrix products, arithmetic and copies ran while one was open for 1% of the time, Pallas kernels for 0%

commit v1 on v0

v1 whole, which is shorter than its diff:
```python
import jax
import jax.numpy as jnp
from jax import lax
from jax.sharding import PartitionSpec as P


def passed_along(value, axis, steps):
    count = lax.axis_size(axis)
    pairs = [(source, (source + steps) % count) for source in range(count)]
    return lax.ppermute(value, axis, pairs)


def other_core(value):
    count = lax.axis_size("expert")
    return lax.ppermute(value, "expert", [(d, d ^ 1) for d in range(count)])


def slot_onehot(route_ids, experts, capacity):
    rows = route_ids.shape[0]
    ids = jnp.arange(experts, dtype=jnp.int32)
    named = jnp.any(route_ids[:, :, None] == ids[None, None, :], axis=1)
    earlier = jnp.arange(rows)[:, None] > jnp.arange(rows)[None, :]
    position = jnp.dot(
        earlier.astype(jnp.bfloat16), named.astype(jnp.bfloat16), preferred_element_type=jnp.float32
    )
    position = jnp.where(named, position, -1.0).T
    slots = jnp.arange(capacity, dtype=jnp.float32)
    onehot = position[:, None, :] == slots[None, :, None]
    return named, onehot.reshape(experts * capacity, rows)


def body(flight, norm_gain, router, w_gate, w_up, w_down, routes):
    rows_local = flight.shape[1]
    model_width = flight.shape[2]
    experts = router.shape[2]
    top_count = routes.shape[3]
    capacity = 2 * min(rows_local // 2, 3 * rows_local * top_count // (4 * experts))
    count = lax.axis_size("expert")
    groups = [list(range(core, count, 2)) for core in range(2)]
    gates = (w_gate[0], other_core(w_gate[0]))
    ups = (w_up[0], other_core(w_up[0]))
    downs = (w_down[0], other_core(w_down[0]))
    current = flight[0]
    for step_index in range(routes.shape[1]):
        float_state = current.astype(jnp.float32)
        normed = (
            float_state
            * lax.rsqrt(jnp.mean(float_state * float_state, axis=-1, keepdims=True) + 1e-06)
            * norm_gain[0][None, :]
        ).astype(jnp.bfloat16)
        named, onehot = slot_onehot(routes[0, step_index], experts, capacity)
        outgoing = jnp.dot(
            onehot.astype(jnp.bfloat16), normed, preferred_element_type=jnp.float32
        ).astype(jnp.bfloat16)
        arrived = lax.all_to_all(
            outgoing.reshape(experts, capacity, model_width),
            "expert",
            split_axis=0,
            concat_axis=0,
            tiled=True,
            axis_index_groups=groups,
        ).reshape(experts * capacity, model_width)
        logits = jnp.dot(normed, router[0], preferred_element_type=jnp.float32)
        raised = jnp.where(named, jnp.exp(logits), 0.0)
        mix_weight = raised / jnp.sum(raised, axis=1, keepdims=True)
        spread = jnp.where(
            onehot.reshape(experts, capacity, rows_local), mix_weight.T[:, None, :], 0.0
        ).reshape(experts * capacity, rows_local)
        spread_high = spread.astype(jnp.bfloat16)
        spread_low = (spread - spread_high.astype(jnp.float32)).astype(jnp.bfloat16)
        total = 0.0
        for gate, up, down in zip(gates, ups, downs):
            gate_act = jnp.dot(arrived, gate, preferred_element_type=jnp.float32)
            up_act = jnp.dot(arrived, up, preferred_element_type=jnp.float32)
            hidden = (jax.nn.silu(gate_act) * up_act).astype(jnp.bfloat16)
            total = total + jnp.dot(hidden, down, preferred_element_type=jnp.float32)
        returned = lax.all_to_all(
            total.astype(jnp.bfloat16).reshape(experts, capacity, model_width),
            "expert",
            split_axis=0,
            concat_axis=0,
            tiled=True,
            axis_index_groups=groups,
        ).reshape(experts * capacity, model_width)
        down_axis = (((0,), (0,)), ((), ()))
        moe = lax.dot_general(
            spread_high, returned, down_axis, preferred_element_type=jnp.float32
        ) + lax.dot_general(spread_low, returned, down_axis, preferred_element_type=jnp.float32)
        current = (float_state + moe).astype(jnp.bfloat16)
        current = passed_along(current, "pipe", 1)
    return current[None]


def solution(mesh):
    return jax.shard_map(
        body,
        mesh=mesh,
        in_specs=(
            P("pipe", "expert", None),
            P("pipe", None),
            P("pipe", None, None),
            P("pipe", None, "expert"),
            P("pipe", None, "expert"),
            P("pipe", "expert", None),
            P("pipe", None, "expert", None),
        ),
        out_specs=P("pipe", "expert", None),
        check_vma=False,
    )
```

time: 512 us -> 296 us (0.58); the launches traced: 503 us -> 295 us
  blocking collectives: 153 us -> 42.1 us
  local copies, waits for them, and re-layouts: 57.7 us -> 2.74 us
  other arithmetic: 52.8 us -> 2.06 us
  matrix products: 28 us -> 67 us
  waiting for transfers between devices: 189 us -> 158 us
    all_to_all x2 -> x1, blocking collectives: 153 us -> 42.1 us  [body(): lax.all_to_all(outgoing.reshape(experts, capacity, model_width), 'expert'...]
    dot_general x6 -> x16, matrix products: 24.7 us -> 63.6 us  [the longest x4 38.2 us: body(): total = total + jnp.dot(hidden, down, preferred_element_type=jnp.float32)]
    gather x4 -> x0, local copies, waits for them, and re-layouts: 34.8 us -> none  [the longest x2 19.7 us: build_slots(): return (slot_index, jnp.take(padded, slot_table, axis=0))]
    all_to_all x2 -> x3, waiting for transfers between devices: 135 us -> 102 us  [the longest x2 66.6 us: body(): lax.all_to_all(total.astype(jnp.bfloat16).reshape(experts, capacity, mode...]
    convert_element_type x10 -> x0, other arithmetic: 25.2 us -> none  [the longest x2 11.7 us: body(): (paired[:, 0].astype(jnp.float32) + paired[:, 1].astype(jnp.float32)).ast...]
    reduce_sum x8 -> x0, other arithmetic: 17.8 us -> none  [the longest x2 17.6 us: body(): moe = jnp.sum(mix_weight[:, :, None] * gathered.astype(jnp.float32), axis=1)]
    convert_element_type x2 -> x0, local copies, waits for them, and re-layouts: 12 us -> none  [body(): moe = jnp.sum(mix_weight[:, :, None] * gathered.astype(jnp.float32), axis=1)]
    all_to_all x2 -> x3, starting transfers between devices: 19.7 us -> 21.7 us  [the longest x2 14.4 us: body(): lax.all_to_all(total.astype(jnp.bfloat16).reshape(experts, capacity, mode...]
  transfers between devices with their start and end apart: 4 -> 8, of which waited for: 4 -> 5; matrix products, arithmetic and copies ran while one was open for 1% -> 7% of each run, Pallas kernels for 0% -> 0%
where the time goes in v1:
time: 296 us; the launch traced here: 295 us
  waiting for transfers between devices  158 us (53%)
  matrix products  67 us (23%)
  blocking collectives  42.1 us (14%)
  starting transfers between devices  23.5 us (8%)
    all_to_all x2, waiting for transfers between devices, body(): lax.all_to_all(total.astype(jnp.bfloat16).reshape(experts, capacity, mode...  66.6 us
    ppermute x2, waiting for transfers between devices, passed_along(): return lax.ppermute(value, axis, pairs)  55.6 us
    all_to_all x1, blocking collectives, body(): lax.all_to_all(outgoing.reshape(experts, capacity, model_width), 'expert'...  42.1 us
    dot_general x4, matrix products, body(): total = total + jnp.dot(hidden, down, preferred_element_type=jnp.float32)  38.2 us
    all_to_all x1, waiting for transfers between devices, body(): lax.all_to_all(outgoing.reshape(experts, capacity, model_width), 'expert'...  35.6 us
    dot_general x4, matrix products, body(): gate_act = jnp.dot(arrived, gate, preferred_element_type=jnp.float32)  16.1 us
    all_to_all x2, starting transfers between devices, body(): lax.all_to_all(total.astype(jnp.bfloat16).reshape(experts, capacity, mode...  14.4 us
    all_to_all x1, starting transfers between devices, body(): lax.all_to_all(outgoing.reshape(experts, capacity, model_width), 'expert'...  7.32 us
  transfers between devices with their start and end apart: 8, of which 5 were waited for; matrix products, arithmetic and copies ran while one was open for 7% of the time, Pallas kernels for 0%

profile of v1, /device:TPU:12, one launch (start us, length us, event | category | flops | bytes accessed | tf_op | source)
XLA Modules:
  0.0 295.4 jit_solution(1241940628910553525)
XLA Ops:
  0.0 0.7 slice_bitcast_fusion.1
  0.9 1.5 fusion.7
  2.5 3.9 %convolution_convert_fusion.1 = bf16[384,4096]{1,0:T(8,128)(2,1)} fusion(pred[384,128]{1,0:T(8,128)(4,1)S(1)} %bitcast.126, bf16[1,128,4096]{2,1,0:T(8,128)(2,1)} %param.7, f32[4096]{0:T(1024)} %bitcast.127, f32[128]{0:T(128)S(1)} %add_rsqrt_fusion.1), kind=kOutput, calls=%fused_computation.3 | convolution fusion | flops 406323200 | bytes 4260352 | tf_op jit(solution)/shard_map/dot_general | solution.py:52
  6.4 7.3 %all-to-all-start = ((bf16[8,48,4096]{2,1,0:T(8,128)(2,1)}), bf16[8,48,4096]{2,1,0:T(8,128)(2,1)S(1)}, u32[]{:S(2)}, u32[]{:S(2)}) async-start(bf16[8,48,4096]{2,1,0:T(8,128)(2,1)} %bitcast.121), calls=%async_computation | async-start | bytes 6291456 | tf_op jit(solution)/shard_map/all_to_all | solution.py:55
  13.7 0.5 collective-permute-start.1
  14.2 35.6 %all-to-all-done = bf16[8,48,4096]{2,1,0:T(8,128)(2,1)S(1)} async-done(((bf16[8,48,4096]{2,1,0:T(8,128)(2,1)}), bf16[8,48,4096]{2,1,0:T(8,128)(2,1)S(1)}, u32[]{:S(2)}, u32[]{:S(2)}) %all-to-all-start) | async-done | bytes 3145760 | tf_op jit(solution)/shard_map/all_to_all | solution.py:55
  49.8 4.5 %fusion.66 = f32[384,384]{1,0:T(8,128)} fusion(bf16[384,4096]{1,0:T(8,128)(2,1)S(1)} %bitcast.111, bf16[1,4096,384]{2,1,0:T(8,128)(2,1)} %param.10), kind=kOutput, calls=%fused_computation.96 | convolution fusion | flops 1207959552 | bytes 6881280 | tf_op jit(solution)/shard_map/dot_general | solution.py:73
  54.3 9.2 %fusion.16 = f32[384,4096]{1,0:T(8,128)} fusion(bf16[384,4096]{1,0:T(8,128)(2,1)S(1)} %bitcast.112, f32[384,384]{1,0:T(8,128)} %fusion.66, bf16[1,384,4096]{2,1,0:T(8,128)(2,1)} %param.12, bf16[1,4096,384]{2,1,0:T(8,128)(2,1)} %param.11), kind=kOutput, calls=%fused_computation.30 | convolution fusion | flops 2416803840 | bytes 16318464 | tf_op jit(solution)/shard_map/dot_general | solution.py:76
  63.5 4.5 %fusion.80 = f32[384,384]{1,0:T(8,128)} fusion(bf16[384,4096]{1,0:T(8,128)(2,1)S(1)} %bitcast.113, bf16[4096,384]{1,0:T(8,128)(2,1)} %collective-permute-done), kind=kOutput, calls=%fused_computation.108 | convolution fusion | flops 1207959552 | bytes 6881280 | tf_op jit(solution)/shard_map/dot_general | solution.py:73
  68.0 10.0 %add_convert_fusion.1 = bf16[384,4096]{1,0:T(8,128)(2,1)} fusion(f32[384,4096]{1,0:T(8,128)} %fusion.16, bf16[384,4096]{1,0:T(8,128)(2,1)} %collective-permute-done.2, f32[384,384]{1,0:T(8,128)} %fusion.80, bf16[384,4096]{1,0:T(8,128)(2,1)S(1)} %bitcast.114, bf16[4096,384]{1,0:T(8,128)(2,1)} %collective-permute-done.1), kind=kOutput, calls=%fused_computation.1 | convolution fusion | flops 2419949568 | bytes 19464192 | tf_op jit(solution)/shard_map/dot_general | solution.py:76
  77.9 7.3 %all-to-all-start.1 = ((bf16[8,48,4096]{2,1,0:T(8,128)(2,1)}), bf16[8,48,4096]{2,1,0:T(8,128)(2,1)S(1)}, u32[]{:S(2)}, u32[]{:S(2)}) async-start(bf16[8,48,4096]{2,1,0:T(8,128)(2,1)} %bitcast.120), calls=%async_computation.1 | async-start | bytes 6291456 | tf_op jit(solution)/shard_map/all_to_all | solution.py:77
  85.2 1.7 select_reduce_fusion.1
  86.9 33.7 %all-to-all-done.1 = bf16[8,48,4096]{2,1,0:T(8,128)(2,1)S(1)} async-done(((bf16[8,48,4096]{2,1,0:T(8,128)(2,1)}), bf16[8,48,4096]{2,1,0:T(8,128)(2,1)S(1)}, u32[]{:S(2)}, u32[]{:S(2)}) %all-to-all-start.1) | async-done | bytes 3145760 | tf_op jit(solution)/shard_map/all_to_all | solution.py:77
  120.6 0.8 convolution_bitcast_fusion.2
  121.4 0.5 copy-done.1
  121.9 1.7 fusion.5
  123.6 1.2 collective-permute-start.3
  125.2 28.5 %collective-permute-done.3 = bf16[128,4096]{1,0:T(8,128)(2,1)S(1)} collective-permute-done((bf16[128,4096]{1,0:T(8,128)(2,1)}, bf16[128,4096]{1,0:T(8,128)(2,1)S(1)}, u32[]{:S(2)}, u32[]{:S(2)}) %collective-permute-start.3) | collective-permute-done | bytes 1048608 | tf_op jit(solution)/shard_map/ppermute | solution.py:10
  154.0 1.1 convolution_convert_fusion
  155.0 42.1 %all_to_all.20 = bf16[8,48,4096]{2,1,0:T(8,128)(2,1)S(1)} all-to-all(bf16[8,48,4096]{2,1,0:T(8,128)(2,1)S(1)} %bitcast.122), channel_id=1, replica_groups={{0,2,4,6,8,10,12,14},{1,3,5,7,9,11,13,15},{16,18,20,22,24,26,28,30},{17..., dimensions={0} | all-to-all | bytes 6291456 | tf_op jit(solution)/shard_map/all_to_all | solution.py:55
  197.2 2.6 fusion.64
  199.8 9.1 %fusion.15 = f32[384,4096]{1,0:T(8,128)} fusion(bf16[384,4096]{1,0:T(8,128)(2,1)S(1)} %bitcast.116, f32[384,384]{1,0:T(8,128)} %fusion.64, bf16[1,384,4096]{2,1,0:T(8,128)(2,1)} %param.12, bf16[1,4096,384]{2,1,0:T(8,128)(2,1)} %param.11), kind=kOutput, calls=%fused_computation.29 | convolution fusion | flops 2416803840 | bytes 16318464 | tf_op jit(solution)/shard_map/dot_general | solution.py:76
  209.0 4.5 %fusion.81 = f32[384,384]{1,0:T(8,128)} fusion(bf16[384,4096]{1,0:T(8,128)(2,1)S(1)} %bitcast.117, bf16[4096,384]{1,0:T(8,128)(2,1)} %collective-permute-done), kind=kOutput, calls=%fused_computation.109 | convolution fusion | flops 1207959552 | bytes 6881280 | tf_op jit(solution)/shard_map/dot_general | solution.py:73
  213.4 10.0 %add_convert_fusion = bf16[384,4096]{1,0:T(8,128)(2,1)} fusion(f32[384,4096]{1,0:T(8,128)} %fusion.15, bf16[384,4096]{1,0:T(8,128)(2,1)} %collective-permute-done.2, f32[384,384]{1,0:T(8,128)} %fusion.81, bf16[384,4096]{1,0:T(8,128)(2,1)S(1)} %bitcast.118, bf16[4096,384]{1,0:T(8,128)(2,1)} %collective-permute-done.1), kind=kOutput, calls=%fused_computation | convolution fusion | flops 2419949568 | bytes 19464192 | tf_op jit(solution)/shard_map/dot_general | solution.py:76
  223.4 7.1 %all-to-all-start.3 = ((bf16[8,48,4096]{2,1,0:T(8,128)(2,1)}), bf16[8,48,4096]{2,1,0:T(8,128)(2,1)S(1)}, u32[]{:S(2)}, u32[]{:S(2)}) async-start(bf16[8,48,4096]{2,1,0:T(8,128)(2,1)} %bitcast.119), calls=%async_computation.3 | async-start | bytes 6291456 | tf_op jit(solution)/shard_map/all_to_all | solution.py:77
  230.5 1.7 select_reduce_fusion
  232.2 32.9 %all-to-all-done.3 = bf16[8,48,4096]{2,1,0:T(8,128)(2,1)S(1)} async-done(((bf16[8,48,4096]{2,1,0:T(8,128)(2,1)}), bf16[8,48,4096]{2,1,0:T(8,128)(2,1)S(1)}, u32[]{:S(2)}, u32[]{:S(2)}) %all-to-all-start.3) | async-done | bytes 3145760 | tf_op jit(solution)/shard_map/all_to_all | solution.py:77
  265.1 0.8 convolution_bitcast_fusion
  265.9 0.5 copy-done.3
  266.3 0.8 fusion.4
  267.2 27.2 %collective-permute-done.4 = bf16[128,4096]{1,0:T(8,128)(2,1)S(1)} collective-permute-done((bf16[128,4096]{1,0:T(8,128)(2,1)S(1)}, bf16[128,4096]{1,0:T(8,128)(2,1)S(1)}, u32[]{:S(2)}, u32[]{:S(2)}) %collective-permute-start.4) | collective-permute-done | bytes 1048608 | tf_op jit(solution)/shard_map/ppermute | solution.py:10
  294.4 1.0 copy.13
  (29 shorter events, 1.0 us)
Async XLA Ops:
  0.0 85.2 %copy-start = (bf16[1,4096,8]{1,2,0:T(8,128)(2,1)S(1)}, bf16[1,4096,8]{1,2,0:T(8,128)(2,1)}, u32[]{:S(2)}) copy-start(bf16[1,4096,8]{1,2,0:T(8,128)(2,1)} %param.9) | copy-start | bytes 196612
  6.4 43.4 %all-to-all-start = ((bf16[8,48,4096]{2,1,0:T(8,128)(2,1)}), bf16[8,48,4096]{2,1,0:T(8,128)(2,1)S(1)}, u32[]{:S(2)}, u32[]{:S(2)}) async-start(bf16[8,48,4096]{2,1,0:T(8,128)(2,1)} %bitcast.121), calls=%async_computation | async-start | bytes 6291456 | tf_op jit(solution)/shard_map/all_to_all | solution.py:55
  13.7 49.8 %collective-permute-start = (bf16[4096,384]{1,0:T(8,128)(2,1)}, bf16[4096,384]{1,0:T(8,128)(2,1)}, u32[]{:S(2)}, u32[]{:S(2)}) collective-permute-start(bf16[4096,384]{1,0:T(8,128)(2,1)} %bitcast.131), channel_id=1, source_target_pairs={{0,1},{1,0},{2,3},{3,2},{4,5},{5,4},{6,7},{7,6},{8,9},{9,8},{10,11... | collective-permute-start | bytes 9437192 | tf_op jit(solution)/shard_map/ppermute | solution.py:15
  13.7 54.2 %collective-permute-start.1 = (bf16[4096,384]{1,0:T(8,128)(2,1)}, bf16[4096,384]{1,0:T(8,128)(2,1)}, u32[]{:S(2)}, u32[]{:S(2)}) collective-permute-start(bf16[4096,384]{1,0:T(8,128)(2,1)} %bitcast.124), channel_id=1, source_target_pairs={{0,1},{1,0},{2,3},{3,2},{4,5},{5,4},{6,7},{7,6},{8,9},{9,8},{10,11... | collective-permute-start | bytes 9437192 | tf_op jit(solution)/shard_map/ppermute | solution.py:15
  14.2 53.7 %collective-permute-start.2 = (bf16[384,4096]{1,0:T(8,128)(2,1)}, bf16[384,4096]{1,0:T(8,128)(2,1)}, u32[]{:S(2)}, u32[]{:S(2)}) collective-permute-start(bf16[384,4096]{1,0:T(8,128)(2,1)} %bitcast.123), channel_id=1, source_target_pairs={{0,1},{1,0},{2,3},{3,2},{4,5},{5,4},{6,7},{7,6},{8,9},{9,8},{10,11... | collective-permute-start | bytes 9437192 | tf_op jit(solution)/shard_map/ppermute | solution.py:15
  77.9 7.3 %copy-start.4 = (f32[1,4096]{1,0:T(1,128)S(1)}, f32[1,4096]{1,0:T(1,128)}, u32[]{:S(2)}) copy-start(f32[1,4096]{1,0:T(1,128)} %param.8) | copy-start | bytes 49156
  77.9 42.7 %all-to-all-start.1 = ((bf16[8,48,4096]{2,1,0:T(8,128)(2,1)}), bf16[8,48,4096]{2,1,0:T(8,128)(2,1)S(1)}, u32[]{:S(2)}, u32[]{:S(2)}) async-start(bf16[8,48,4096]{2,1,0:T(8,128)(2,1)} %bitcast.120), calls=%async_computation.1 | async-start | bytes 6291456 | tf_op jit(solution)/shard_map/all_to_all | solution.py:77
  120.6 1.2 copy-start.1
  123.6 30.0 %collective-permute-start.3 = (bf16[128,4096]{1,0:T(8,128)(2,1)}, bf16[128,4096]{1,0:T(8,128)(2,1)S(1)}, u32[]{:S(2)}, u32[]{:S(2)}) collective-permute-start(bf16[128,4096]{1,0:T(8,128)(2,1)} %fusion.5), channel_id=1, source_target_pairs={{0,16},{16,32},{32,48},{48,64},{64,80},{80,96},{96,112},{112,128},... | collective-permute-start | bytes 3145736 | tf_op jit(solution)/shard_map/ppermute | solution.py:10
  153.7 1.4 copy-start.2
  155.0 42.1 %copy-start.5 = (bf16[1,4096,384]{2,1,0:T(8,128)(2,1)S(1)}, bf16[1,4096,384]{2,1,0:T(8,128)(2,1)}, u32[]{:S(2)}) copy-start(bf16[1,4096,384]{2,1,0:T(8,128)(2,1)} %param.10) | copy-start | bytes 9437188
  223.4 41.7 %all-to-all-start.3 = ((bf16[8,48,4096]{2,1,0:T(8,128)(2,1)}), bf16[8,48,4096]{2,1,0:T(8,128)(2,1)S(1)}, u32[]{:S(2)}, u32[]{:S(2)}) async-start(bf16[8,48,4096]{2,1,0:T(8,128)(2,1)} %bitcast.119), calls=%async_computation.3 | async-start | bytes 6291456 | tf_op jit(solution)/shard_map/all_to_all | solution.py:77
  265.1 1.2 copy-start.3
  267.1 27.3 %collective-permute-start.4 = (bf16[128,4096]{1,0:T(8,128)(2,1)S(1)}, bf16[128,4096]{1,0:T(8,128)(2,1)S(1)}, u32[]{:S(2)}, u32[]{:S(2)}) collective-permute-start(bf16[128,4096]{1,0:T(8,128)(2,1)S(1)} %fusion.4), channel_id=1, source_target_pairs={{0,16},{16,32},{32,48},{48,64},{64,80},{80,96},{96,112},{112,128},... | collective-permute-start | bytes 3145736 | tf_op jit(solution)/shard_map/ppermute | solution.py:10

commit v2 on v1

v2 whole, which is shorter than its diff:
```python
import functools

import jax
import jax.numpy as jnp
from jax import lax
from jax.experimental import pallas as pl
from jax.experimental.pallas import tpu as pltpu
from jax.sharding import PartitionSpec as P

DEEP = 1024
WIDE = 1024


def dot(a, b):
    return jnp.dot(a, b, preferred_element_type=jnp.float32)


def split_high_low(value):
    high = value.astype(jnp.bfloat16)
    return high, (value - high.astype(jnp.float32)).astype(jnp.bfloat16)


def to_core(value):
    count = lax.axis_size("expert")
    return lax.ppermute(value, "expert", [(d, d ^ 1) for d in range(count)])


def to_next(value):
    sections = lax.axis_size("pipe")
    return lax.ppermute(value, "pipe", [(p, (p + 1) % sections) for p in range(sections)])


def exchanged(value, experts):
    count = lax.axis_size("expert")
    groups = [list(range(core, count, 2)) for core in range(2)]
    slots, width = value.shape
    swapped = lax.all_to_all(
        value.reshape(experts, slots // experts, width),
        "expert",
        split_axis=0,
        concat_axis=0,
        tiled=True,
        axis_index_groups=groups,
    )
    return swapped.reshape(slots, width)


def expert_kernel(
    x_ref, g0, g1, u0, u1, d0, d1, out_ref, x, w_in, w_out, acc, hidden, outs,
    x_sem, in_sem, down_sem, out_sem,
):
    width = x.shape[1]
    half = g0.shape[1]
    units = 2 * half
    deep_count, wide_count = width // DEEP, width // WIDE

    def x_copy(k):
        cut = pl.ds(k * DEEP, DEEP)
        return pltpu.make_async_copy(x_ref.at[:, cut], x.at[:, cut], x_sem.at[k])

    def in_copy(k, j):
        source = (g0, g1, u0, u1)[j]
        cut = pl.ds(k * DEEP, DEEP)
        target = w_in.at[cut, pl.ds(j * half, half)]
        return pltpu.make_async_copy(source.at[cut, :], target, in_sem.at[k, j])

    def down_copy(n, j):
        cut = pl.ds(n * WIDE, WIDE)
        target = w_out.at[pl.ds(j * half, half), cut]
        return pltpu.make_async_copy((d0, d1)[j].at[:, cut], target, down_sem.at[n, j])

    def out_copy(n):
        cut = pl.ds(n * WIDE, WIDE)
        return pltpu.make_async_copy(outs.at[:, cut], out_ref.at[:, cut], out_sem.at[n])

    for k in range(deep_count):
        x_copy(k).start()
        for j in range(4):
            in_copy(k, j).start()
    for n in range(wide_count):
        for j in range(2):
            down_copy(n, j).start()
    for k in range(deep_count):
        x_copy(k).wait()
        for j in range(4):
            in_copy(k, j).wait()
        cut = slice(k * DEEP, (k + 1) * DEEP)
        product = dot(x[:, cut], w_in[cut, :])
        if k == 0:
            acc[...] = product
        else:
            acc[...] += product
    gate, up = acc[:, :units], acc[:, units:]
    hidden[...] = (gate / (1.0 + jnp.exp(-gate)) * up).astype(jnp.bfloat16)
    for n in range(wide_count):
        for j in range(2):
            down_copy(n, j).wait()
        cut = slice(n * WIDE, (n + 1) * WIDE)
        outs[:, cut] = dot(hidden[...], w_out[:, cut]).astype(jnp.bfloat16)
        out_copy(n).start()
    for n in range(wide_count):
        out_copy(n).wait()


def expert_rows(rows, gates, ups, downs):
    slots, width = rows.shape
    half = gates[0].shape[1]
    units = 2 * half
    deep_count, wide_count = width // DEEP, width // WIDE
    anywhere = pl.BlockSpec(memory_space=pl.ANY)
    return pl.pallas_call(
        expert_kernel,
        out_shape=jax.ShapeDtypeStruct((slots, width), jnp.bfloat16),
        in_specs=[anywhere] * 7,
        out_specs=anywhere,
        scratch_shapes=[
            pltpu.VMEM((slots, width), jnp.bfloat16),
            pltpu.VMEM((width, 2 * units), jnp.bfloat16),
            pltpu.VMEM((units, width), jnp.bfloat16),
            pltpu.VMEM((slots, 2 * units), jnp.float32),
            pltpu.VMEM((slots, units), jnp.bfloat16),
            pltpu.VMEM((slots, width), jnp.bfloat16),
            pltpu.SemaphoreType.DMA((deep_count,)),
            pltpu.SemaphoreType.DMA((deep_count, 4)),
            pltpu.SemaphoreType.DMA((wide_count, 2)),
            pltpu.SemaphoreType.DMA((wide_count,)),
        ],
        compiler_params=pltpu.CompilerParams(vmem_limit_bytes=44 * 1024 * 1024),
        cost_estimate=pl.CostEstimate(
            flops=6 * slots * width * units,
            bytes_accessed=2 * (3 * width * units + 2 * slots * width),
            transcendentals=slots * units,
        ),
    )(rows, *gates, *ups, *downs)


def route_slots(route_ids, experts, capacity):
    rows = route_ids.shape[0]
    ids = jnp.arange(experts, dtype=jnp.int32)
    named = jnp.any(route_ids[:, :, None] == ids[None, None, :], axis=1)
    earlier = jnp.arange(rows)[:, None] > jnp.arange(rows)[None, :]
    position = dot(earlier.astype(jnp.bfloat16), named.astype(jnp.bfloat16))
    position = jnp.where(named, position, -1.0).T
    slots = jnp.arange(capacity, dtype=jnp.float32)
    onehot = position[:, None, :] == slots[None, :, None]
    return named, onehot


def body(flight, norm_gain, router, w_gate, w_up, w_down, routes):
    rows = flight.shape[1]
    experts = router.shape[2]
    ticks = routes.shape[1]
    top_count = routes.shape[3]
    capacity = 2 * min(rows // 2, 3 * rows * top_count // (4 * experts))
    slot_count = experts * capacity
    gates = (w_gate[0], to_core(w_gate[0]))
    ups = (w_up[0], to_core(w_up[0]))
    downs = (w_down[0], to_core(w_down[0]))

    current = flight[0]
    for tick in range(ticks):
        named, onehot = route_slots(routes[0, tick], experts, capacity)
        pick = onehot.reshape(slot_count, rows).astype(jnp.bfloat16)
        float_state = current.astype(jnp.float32)
        normed = (
            float_state
            * lax.rsqrt(jnp.mean(float_state * float_state, axis=-1, keepdims=True) + 1e-06)
            * norm_gain[0][None, :]
        ).astype(jnp.bfloat16)
        normed = lax.optimization_barrier(normed)
        arrived = exchanged(dot(pick, normed).astype(jnp.bfloat16), experts)
        logits = dot(normed, router[0])
        raised = jnp.where(named, jnp.exp(logits), 0.0)
        mix_weight = raised / jnp.sum(raised, axis=1, keepdims=True)
        spread = jnp.where(onehot, mix_weight.T[:, None, :], 0.0).reshape(slot_count, rows).T
        spread_high, spread_low = split_high_low(spread)
        outs = expert_rows(arrived, gates, ups, downs)
        returned = exchanged(outs, experts)
        moe = dot(spread_high, returned) + dot(spread_low, returned)
        current = to_next((float_state + moe).astype(jnp.bfloat16))
    return current[None]


def solution(mesh):
    return jax.shard_map(
        body,
        mesh=mesh,
        in_specs=(
            P("pipe", "expert", None),
            P("pipe", None),
            P("pipe", None, None),
            P("pipe", None, "expert"),
            P("pipe", None, "expert"),
            P("pipe", "expert", None),
            P("pipe", None, "expert", None),
        ),
        out_specs=P("pipe", "expert", None),
        check_vma=False,
    )
```

time: 296 us -> 268 us (0.905)
  matrix products: 67 us -> 12.3 us
  blocking collectives: 42.1 us -> 85.9 us
  waiting for transfers between devices: 158 us -> 123 us
  Pallas kernels: 0 us -> 22.9 us
  starting transfers between devices: 23.5 us -> 17.3 us
    dot_general x18 -> x10, matrix products: 67 us -> 12.3 us  [dot(): return jnp.dot(a, b, preferred_element_type=jnp.float32)]
    all_to_all x1 -> x2, blocking collectives: 42.1 us -> 85.9 us  [exchanged(): lax.all_to_all(value.reshape(experts, slots // experts, width), 'expert',...]
    all_to_all x3 -> x2, waiting for transfers between devices: 102 us -> 66.8 us  [exchanged(): lax.all_to_all(value.reshape(experts, slots // experts, width), 'expert',...]
    pallas_call x0 -> x2, Pallas kernels: none -> 22.9 us  [expert_rows(): pl.pallas_call(expert_kernel, out_shape=jax.ShapeDtypeStruct((slots, widt...]
    all_to_all x3 -> x2, starting transfers between devices: 21.7 us -> 15.1 us  [exchanged(): lax.all_to_all(value.reshape(experts, slots // experts, width), 'expert',...]
  transfers between devices with their start and end apart: 8 -> 7, of which waited for: 5 -> 4; matrix products, arithmetic and copies ran while one was open for 7% -> 3% of each run, Pallas kernels for 0% -> 0%
where the time goes in v2:
time: 268 us
  waiting for transfers between devices  123 us (46%)
  blocking collectives  85.9 us (32%)
  Pallas kernels  22.9 us (9%)
  starting transfers between devices  17.3 us (6%)
  matrix products  12.3 us (5%)
  other arithmetic  4.36 us (2%)
    all_to_all x2, blocking collectives, exchanged(): lax.all_to_all(value.reshape(experts, slots // experts, width), 'expert',...  85.9 us
    all_to_all x2, waiting for transfers between devices, exchanged(): lax.all_to_all(value.reshape(experts, slots // experts, width), 'expert',...  66.8 us
    ppermute x2, waiting for transfers between devices, to_next(): lax.ppermute(value, 'pipe', [(p, (p + 1) % sections) for p in range(secti...  55.8 us
    pallas_call x2, Pallas kernels, expert_rows(): pl.pallas_call(expert_kernel, out_shape=jax.ShapeDtypeStruct((slots, widt...  22.9 us
    all_to_all x2, starting transfers between devices, exchanged(): lax.all_to_all(value.reshape(experts, slots // experts, width), 'expert',...  15.1 us
    dot_general x10, matrix products, dot(): return jnp.dot(a, b, preferred_element_type=jnp.float32)  12.3 us
  transfers between devices with their start and end apart: 7, of which 4 were waited for; matrix products, arithmetic and copies ran while one was open for 3% of the time, Pallas kernels for 0%

profile of v2, /device:TPU:12, one launch (start us, length us, event | category | flops | bytes accessed | tf_op | source)
XLA Modules:
  0.0 267.8 jit_solution(17906782319760703565)
XLA Ops:
  0.0 0.5 collective-permute-start.1
  0.6 0.7 slice_bitcast_fusion
  1.3 1.5 fusion.7
  2.8 0.1 convolution_select_fusion.1
  3.0 1.6 fusion.9
  4.6 0.1 convolution_select_fusion
  4.8 0.1 bitcast_compare_fusion
  4.9 1.0 convolution_convert_fusion.1
  5.9 44.1 %all_to_all.20 = bf16[8,48,4096]{2,1,0:T(8,128)(2,1)S(1)} all-to-all(bf16[8,48,4096]{2,1,0:T(8,128)(2,1)S(1)} %bitcast.114), channel_id=1, replica_groups={{0,2,4,6,8,10,12,14},{1,3,5,7,9,11,13,15},{16,18,20,22,24,26,28,30},{17..., dimensions={0} | all-to-all | bytes 6291456 | tf_op jit(solution)/shard_map/all_to_all | solution.py:37
  50.0 11.4 %shard_map.73 = bf16[384,4096]{1,0:T(8,128)(2,1)} custom-call(bf16[384,4096]{1,0:T(8,128)(2,1)S(1)} %bitcast.107, bf16[4096,384]{1,0:T(8,128)(2,1)S(1)} %bitcast.110, bf16[4096,384]{1,0:T(8,128)(2,1)} %collective-permute-done.g1, bf16[4096,384]{1,0:T(8,128)(2,1)} %bitcast.120, bf16[4096,384]{1,0:T(8,128)(2,1)} %collective-permute-done.1.u1, ...), custom_call_target="tpu_custom_call" | custom-call | flops 7247757312 | bytes 25165824 | tf_op jit(solution)/shard_map/pallas_call | solution.py:111
  61.5 7.9 %all-to-all-start.1 = ((bf16[8,48,4096]{2,1,0:T(8,128)(2,1)}), bf16[8,48,4096]{2,1,0:T(8,128)(2,1)}, u32[]{:S(2)}, u32[]{:S(2)}) async-start(bf16[8,48,4096]{2,1,0:T(8,128)(2,1)} %bitcast.15), calls=%async_computation.1 | async-start | bytes 6291456 | tf_op jit(solution)/shard_map/all_to_all | solution.py:37
  69.4 1.6 select_reduce_fusion.1
  71.1 0.1 fusion.11
  71.3 34.1 %all-to-all-done.1 = bf16[8,48,4096]{2,1,0:T(8,128)(2,1)} async-done(((bf16[8,48,4096]{2,1,0:T(8,128)(2,1)}), bf16[8,48,4096]{2,1,0:T(8,128)(2,1)}, u32[]{:S(2)}, u32[]{:S(2)}) %all-to-all-start.1) | async-done | bytes 3145760 | tf_op jit(solution)/shard_map/all_to_all | solution.py:37
  105.4 2.7 %fusion.18 = f32[128,4096]{1,0:T(8,128)S(1)} fusion(bf16[128,384]{0,1:T(8,128)(2,1)S(1)} %fusion.11, bf16[384,4096]{1,0:T(8,128)(2,1)} %bitcast.16), kind=kOutput, calls=%fused_computation.49 | convolution fusion | flops 402653184 | bytes 5341184 | tf_op jit(solution)/shard_map/dot_general | solution.py:15
  108.1 2.7 fusion.2
  110.8 1.5 collective-permute-start.3
  112.3 28.6 %collective-permute-done.3 = bf16[128,4096]{1,0:T(8,128)(2,1)S(1)} collective-permute-done((bf16[128,4096]{1,0:T(8,128)(2,1)S(1)}, bf16[128,4096]{1,0:T(8,128)(2,1)S(1)}, u32[]{:S(2)}, u32[]{:S(2)}) %collective-permute-start.3) | collective-permute-done | bytes 1048608 | tf_op jit(solution)/shard_map/ppermute | solution.py:30
  140.9 0.3 fusion.4
  141.2 0.3 fusion.6
  141.6 1.0 convolution_convert_fusion
  142.5 41.8 %all_to_all.21 = bf16[8,48,4096]{2,1,0:T(8,128)(2,1)S(1)} all-to-all(bf16[8,48,4096]{2,1,0:T(8,128)(2,1)S(1)} %bitcast.115), channel_id=1, replica_groups={{0,2,4,6,8,10,12,14},{1,3,5,7,9,11,13,15},{16,18,20,22,24,26,28,30},{17..., dimensions={0} | all-to-all | bytes 6291456 | tf_op jit(solution)/shard_map/all_to_all | solution.py:37
  184.4 11.4 %shard_map.74 = bf16[384,4096]{1,0:T(8,128)(2,1)} custom-call(bf16[384,4096]{1,0:T(8,128)(2,1)S(1)} %bitcast.108, bf16[4096,384]{1,0:T(8,128)(2,1)S(1)} %bitcast.111, bf16[4096,384]{1,0:T(8,128)(2,1)} %collective-permute-done.g1, bf16[4096,384]{1,0:T(8,128)(2,1)} %bitcast.121, bf16[4096,384]{1,0:T(8,128)(2,1)} %collective-permute-done.1.u1, ...), custom_call_target="tpu_custom_call" | custom-call | flops 7247757312 | bytes 25165824 | tf_op jit(solution)/shard_map/pallas_call | solution.py:111
  195.8 7.2 %all-to-all-start.3 = ((bf16[8,48,4096]{2,1,0:T(8,128)(2,1)}), bf16[8,48,4096]{2,1,0:T(8,128)(2,1)S(1)}, u32[]{:S(2)}, u32[]{:S(2)}) async-start(bf16[8,48,4096]{2,1,0:T(8,128)(2,1)} %bitcast.25), calls=%async_computation.3 | async-start | bytes 6291456 | tf_op jit(solution)/shard_map/all_to_all | solution.py:37
  203.0 1.6 select_reduce_fusion
  204.6 0.1 fusion.10
  204.9 32.7 %all-to-all-done.3 = bf16[8,48,4096]{2,1,0:T(8,128)(2,1)S(1)} async-done(((bf16[8,48,4096]{2,1,0:T(8,128)(2,1)}), bf16[8,48,4096]{2,1,0:T(8,128)(2,1)S(1)}, u32[]{:S(2)}, u32[]{:S(2)}) %all-to-all-start.3) | async-done | bytes 3145760 | tf_op jit(solution)/shard_map/all_to_all | solution.py:37
  237.6 0.7 fusion.19
  238.3 0.5 copy-done.6
  238.8 0.8 fusion.3
  239.7 27.2 %collective-permute-done.4 = bf16[128,4096]{1,0:T(8,128)(2,1)S(1)} collective-permute-done((bf16[128,4096]{1,0:T(8,128)(2,1)S(1)}, bf16[128,4096]{1,0:T(8,128)(2,1)S(1)}, u32[]{:S(2)}, u32[]{:S(2)}) %collective-permute-start.4) | collective-permute-done | bytes 1048608 | tf_op jit(solution)/shard_map/ppermute | solution.py:30
  266.9 1.0 copy.15
  (30 shorter events, 0.6 us)
Async XLA Ops:
  0.0 69.4 %copy-start = (bf16[1,4096,8]{1,2,0:T(8,128)(2,1)S(1)}, bf16[1,4096,8]{1,2,0:T(8,128)(2,1)}, u32[]{:S(2)}) copy-start(bf16[1,4096,8]{1,2,0:T(8,128)(2,1)} %param.9) | copy-start | bytes 196612
  0.0 50.0 %collective-permute-start = (bf16[4096,384]{1,0:T(8,128)(2,1)}, bf16[4096,384]{1,0:T(8,128)(2,1)}, u32[]{:S(2)}, u32[]{:S(2)}) collective-permute-start(bf16[4096,384]{1,0:T(8,128)(2,1)} %bitcast.109), channel_id=1, source_target_pairs={{0,1},{1,0},{2,3},{3,2},{4,5},{5,4},{6,7},{7,6},{8,9},{9,8},{10,11... | collective-permute-start | bytes 9437192 | tf_op jit(solution)/shard_map/ppermute | solution.py:25
  0.0 50.0 %collective-permute-start.1 = (bf16[4096,384]{1,0:T(8,128)(2,1)}, bf16[4096,384]{1,0:T(8,128)(2,1)}, u32[]{:S(2)}, u32[]{:S(2)}) collective-permute-start(bf16[4096,384]{1,0:T(8,128)(2,1)} %bitcast.119), channel_id=1, source_target_pairs={{0,1},{1,0},{2,3},{3,2},{4,5},{5,4},{6,7},{7,6},{8,9},{9,8},{10,11... | collective-permute-start | bytes 9437192 | tf_op jit(solution)/shard_map/ppermute | solution.py:25
  0.5 49.5 %collective-permute-start.2 = (bf16[384,4096]{1,0:T(8,128)(2,1)}, bf16[384,4096]{1,0:T(8,128)(2,1)}, u32[]{:S(2)}, u32[]{:S(2)}) collective-permute-start(bf16[384,4096]{1,0:T(8,128)(2,1)} %bitcast.122), channel_id=1, source_target_pairs={{0,1},{1,0},{2,3},{3,2},{4,5},{5,4},{6,7},{7,6},{8,9},{9,8},{10,11... | collective-permute-start | bytes 9437192 | tf_op jit(solution)/shard_map/ppermute | solution.py:25
  4.6 1.4 copy-start.2
  5.9 44.1 %copy-start.1 = (bf16[1,4096,384]{2,1,0:T(8,128)(2,1)S(1)}, bf16[1,4096,384]{2,1,0:T(8,128)(2,1)}, u32[]{:S(2)}) copy-start(bf16[1,4096,384]{2,1,0:T(8,128)(2,1)} %param.10) | copy-start | bytes 9437188
  61.5 43.9 %all-to-all-start.1 = ((bf16[8,48,4096]{2,1,0:T(8,128)(2,1)}), bf16[8,48,4096]{2,1,0:T(8,128)(2,1)}, u32[]{:S(2)}, u32[]{:S(2)}) async-start(bf16[8,48,4096]{2,1,0:T(8,128)(2,1)} %bitcast.15), calls=%async_computation.1 | async-start | bytes 6291456 | tf_op jit(solution)/shard_map/all_to_all | solution.py:37
  105.4 2.7 %copy-start.4 = (bf16[1,128,4096]{2,1,0:T(8,128)(2,1)S(1)}, bf16[1,128,4096]{2,1,0:T(8,128)(2,1)}, u32[]{:S(2)}) copy-start(bf16[1,128,4096]{2,1,0:T(8,128)(2,1)} %param.7) | copy-start | bytes 3145732
  108.1 33.1 %copy-start.7 = (f32[1,4096]{1,0:T(1,128)S(1)}, f32[1,4096]{1,0:T(1,128)}, u32[]{:S(2)}) copy-start(f32[1,4096]{1,0:T(1,128)} %param.8) | copy-start | bytes 49156
  110.8 30.1 %collective-permute-start.3 = (bf16[128,4096]{1,0:T(8,128)(2,1)S(1)}, bf16[128,4096]{1,0:T(8,128)(2,1)S(1)}, u32[]{:S(2)}, u32[]{:S(2)}) collective-permute-start(bf16[128,4096]{1,0:T(8,128)(2,1)S(1)} %fusion.2), channel_id=1, source_target_pairs={{0,16},{16,32},{32,48},{48,64},{64,80},{80,96},{96,112},{112,128},... | collective-permute-start | bytes 3145736 | tf_op jit(solution)/shard_map/ppermute | solution.py:30
  140.9 1.6 copy-start.5
  141.5 42.8 %copy-start.3 = (bf16[128,4096]{1,0:T(8,128)(2,1)}, bf16[128,4096]{1,0:T(8,128)(2,1)S(1)}, u32[]{:S(2)}) copy-start(bf16[128,4096]{1,0:T(8,128)(2,1)S(1)} %fusion.6) | copy-start | bytes 3145732
  195.8 41.8 %all-to-all-start.3 = ((bf16[8,48,4096]{2,1,0:T(8,128)(2,1)}), bf16[8,48,4096]{2,1,0:T(8,128)(2,1)S(1)}, u32[]{:S(2)}, u32[]{:S(2)}) async-start(bf16[8,48,4096]{2,1,0:T(8,128)(2,1)} %bitcast.25), calls=%async_computation.3 | async-start | bytes 6291456 | tf_op jit(solution)/shard_map/all_to_all | solution.py:37
  237.6 1.2 copy-start.6
  239.6 27.3 %collective-permute-start.4 = (bf16[128,4096]{1,0:T(8,128)(2,1)S(1)}, bf16[128,4096]{1,0:T(8,128)(2,1)S(1)}, u32[]{:S(2)}, u32[]{:S(2)}) collective-permute-start(bf16[128,4096]{1,0:T(8,128)(2,1)S(1)} %fusion.3), channel_id=1, source_target_pairs={{0,16},{16,32},{32,48},{48,64},{64,80},{80,96},{96,112},{112,128},... | collective-permute-start | bytes 3145736 | tf_op jit(solution)/shard_map/ppermute | solution.py:30
